TPU v7x, 32 devices: a whole 2x2x4 slice. The times are simulated.
32 devices in a mesh: groups: 2 (over y), store: 4 (over z), head: 2 (over x), sub: 2 (over core).
Axes of the slice: x: 2, y: 2, z: 4, core: 2. Of those that a mesh axis runs over, the one named last changes fastest.
Arguments:
- fresh_query: bfloat16 [16, 528, 8192], P(('groups', 'store'), None, ('head', 'sub')), parts along dimension 0, may hold values from -20 to 20
- fresh_keys: bfloat16 [16, 528, 1024], P(('groups', 'store'), None, 'head'), parts along dimension 0, may hold values from -6 to 6
- fresh_values: bfloat16 [16, 528, 1024], P(('groups', 'store'), None, 'head'), parts along dimension 0, may hold values from -24 to 24
- store_keys: bfloat16 [64, 512, 1024], P(('groups', 'store'), 'sub', 'head'), parts along dimension 0, may hold values from -6 to 6
- store_values: bfloat16 [64, 512, 1024], P(('groups', 'store'), 'sub', 'head'), parts along dimension 0, may hold values from -24 to 24
- span_ids: int32 [16, 6], P('groups'), parts along dimension 0, may hold values from 0 to 31, as said below
- span_slot: int32 [64], P('groups'), parts along dimension 0, may hold values from 0 to 31, as said below
- select_pos: int32 [16, 464], P('groups'), parts along dimension 0, may hold values from 0 to 3071, as said below
- ask_len: int32 [16], P('groups'), parts along dimension 0, may hold values from 1 to 64, as said below
Outputs:
- attn_out: bfloat16 [16, 528, 8192], P(('groups', 'store'), None, ('head', 'sub')), parts along dimension 0
There are 2 independent parts, one for each index of `groups`. A program takes and returns all parts, laid end to end along the dimension named above; each array names one. Nothing has to cross between parts.
Inputs may be any that keep to these rules, and one draw needn't show every extreme that they name: `span_ids`: the 6 spans of a request are distinct. Over the 2 requests of one store index (requests s * 2 to s * 2 + 1) all named spans are distinct, and at most 3 of them have slots on any one store index, exactly 3 on some. `span_slot`: A permutation; the span with slot v is held by store index v // 8. `select_pos`: strictly increasing within each request. `ask_len`: some request has 64.
All inputs are finite; a program needn't handle non-finite values.
Results may differ from a plain program's by a relative error of at most 0.0045.
Values may be sent and summed in bfloat16 or wider, within the bound.
A program may use at most 128 MiB of HBM per device.

v0:
```python
import jax
import jax.numpy as jnp
from jax import lax
from jax.sharding import PartitionSpec as P

HD = 128
GROUP = 8
SPAN = 512
NCH = 6
CTX = 3072
SEL = 464
QLEN = 64
ROWS = 528


NEGATIVE = -1e30


def empty_state(kv_used, per_kv):
    return (
        jnp.full((kv_used, per_kv, ROWS), NEGATIVE, jnp.float32),
        jnp.zeros((kv_used, per_kv, ROWS), jnp.float32),
        jnp.zeros((ROWS, kv_used, per_kv, HD), jnp.float32),
    )


def attend_block(carried, query_four, query_pos, block_keys, block_values, key_pos, key_live):
    row_max, totals, weighted = carried
    score_scale = HD ** (-0.5)
    scores = (
        jnp.einsum("rngd,knd->ngrk", query_four, block_keys, preferred_element_type=jnp.float32)
        * score_scale
    )
    allowed = (key_pos[None, :] <= query_pos[:, None]) & key_live[None, :]
    scores = jnp.where(allowed, scores, NEGATIVE)
    new_max = jnp.maximum(row_max, jnp.max(scores, axis=-1))
    powers = jnp.where(allowed, jnp.exp(scores - new_max[..., None]), 0.0)
    factor = jnp.exp(row_max - new_max)
    totals = totals * factor + jnp.sum(powers, axis=-1)
    weights = powers.astype(jnp.bfloat16)
    update = jnp.einsum("ngrk,knd->rngd", weights, block_values, preferred_element_type=jnp.float32)
    weighted = weighted * jnp.transpose(factor, (2, 0, 1))[..., None] + update
    return (new_max, totals, weighted)


def context_pass(carried, query_four, query_pos, ctx_keys, ctx_values, ctx_live):
    kv_used = ctx_keys.shape[1]
    block_keys = ctx_keys.reshape(NCH, SPAN, kv_used, HD)
    block_values = ctx_values.reshape(NCH, SPAN, kv_used, HD)
    block_pos = jnp.arange(CTX, dtype=jnp.int32).reshape(NCH, SPAN)
    block_live = ctx_live.reshape(NCH, SPAN)

    def advance(running, pieces):
        return (
            attend_block(
                running, query_four, query_pos, pieces[0], pieces[1], pieces[2], pieces[3]
            ),
            None,
        )

    carried, unused = lax.scan(advance, carried, (block_keys, block_values, block_pos, block_live))
    return carried


def body(
    fresh_query,
    fresh_keys,
    fresh_values,
    store_keys,
    store_values,
    span_ids,
    span_slot,
    select_pos,
    ask_len,
):
    stores = lax.axis_size("store")
    store_index = lax.axis_index("store")
    core_half = lax.axis_index("sub")
    req_dev = fresh_query.shape[0]
    ch_dev = store_keys.shape[0]
    references = req_dev * NCH
    capacity = (references + stores - 1) // stores
    q_heads = fresh_query.shape[2] // HD
    kv_used = max(q_heads // GROUP, 1)
    per_kv = q_heads // kv_used
    kv_first = core_half * q_heads // GROUP
    slot_ids = span_slot[span_ids].reshape(stores, references)
    owners = slot_ids // ch_dev
    places = slot_ids % ch_dev
    my_owners = lax.dynamic_index_in_dim(owners, store_index, 0, keepdims=False)
    earlier = jnp.arange(references)[None, :] < jnp.arange(references)[:, None]
    my_ranks = jnp.sum((my_owners[:, None] == my_owners[None, :]) & earlier, axis=1)
    flat_spot = my_owners * capacity + my_ranks
    is_mine = owners == store_index
    ranks = jnp.cumsum(is_mine.astype(jnp.int32), axis=1) - 1
    bucket_hit = is_mine[:, None, :] & (ranks[:, None, :] == jnp.arange(capacity)[None, :, None])
    send_place = jnp.sum(jnp.where(bucket_hit, places[:, None, :], 0), axis=2)
    my_pos = lax.dynamic_slice_in_dim(select_pos, store_index * req_dev, req_dev, 0)
    my_len = lax.dynamic_slice_in_dim(ask_len, store_index * req_dev, req_dev, 0)
    prepared = []
    for request in range(req_dev):
        query_four = fresh_query[request].reshape(ROWS, kv_used, per_kv, HD)
        row_keys = lax.dynamic_slice_in_dim(
            fresh_keys[request], kv_first * HD, kv_used * HD, 1
        ).reshape(ROWS, kv_used, HD)
        row_values = lax.dynamic_slice_in_dim(
            fresh_values[request], kv_first * HD, kv_used * HD, 1
        ).reshape(ROWS, kv_used, HD)
        query_pos = jnp.concatenate([my_pos[request], CTX + jnp.arange(QLEN, dtype=jnp.int32)])
        row_live = jnp.arange(ROWS, dtype=jnp.int32) < SEL + my_len[request]
        prepared.append((query_four, row_keys, row_values, query_pos, row_live))
    early_states = []
    for request in range(req_dev):
        query_four, row_keys, row_values, query_pos, row_live = prepared[request]
        early_states.append(
            attend_block(
                empty_state(kv_used, per_kv),
                query_four,
                query_pos,
                row_keys,
                row_values,
                query_pos,
                row_live,
            )
        )
    whole_keys, whole_values = (
        lax.all_gather(store_keys, "sub", axis=1, tiled=True),
        lax.all_gather(store_values, "sub", axis=1, tiled=True),
    )
    arrived = (
        lax.all_to_all(whole_keys[send_place], "store", split_axis=0, concat_axis=0, tiled=True),
        lax.all_to_all(whole_values[send_place], "store", split_axis=0, concat_axis=0, tiled=True),
    )
    page_keys = arrived[0].reshape((stores * capacity,) + arrived[0].shape[2:])[flat_spot]
    page_values = arrived[1].reshape((stores * capacity,) + arrived[1].shape[2:])[flat_spot]
    kv_columns = page_keys.shape[2]
    context_keys = lax.dynamic_slice_in_dim(
        page_keys.reshape(req_dev, CTX, kv_columns), kv_first * HD, kv_used * HD, 2
    )
    context_keys = context_keys.reshape(req_dev, CTX, kv_used, HD)
    context_values = lax.dynamic_slice_in_dim(
        page_values.reshape(req_dev, CTX, kv_columns), kv_first * HD, kv_used * HD, 2
    )
    context_values = context_values.reshape(req_dev, CTX, kv_used, HD)
    outputs = []
    for request in range(req_dev):
        query_four, row_keys, row_values, query_pos, row_live = prepared[request]
        positions = my_pos[request]
        chosen = jnp.zeros((CTX,), jnp.bool_).at[positions].set(True)
        carried = context_pass(
            early_states[request],
            query_four,
            query_pos,
            context_keys[request],
            context_values[request],
            jnp.logical_not(chosen),
        )
        row_max, totals, weighted = carried
        result = weighted / jnp.transpose(totals, (2, 0, 1))[..., None]
        result = jnp.where(row_live[:, None], result.reshape(ROWS, q_heads * HD), 0.0)
        outputs.append(result.astype(jnp.bfloat16))
    return jnp.stack(outputs)


def solution(mesh):
    placed = (
        P(("groups", "store"), None, ("head", "sub")),
        P(("groups", "store"), None, "head"),
        P(("groups", "store"), None, "head"),
        P(("groups", "store"), "sub", "head"),
        P(("groups", "store"), "sub", "head"),
        P("groups", None),
        P("groups"),
        P("groups", None),
        P("groups"),
    )
    return jax.shard_map(
        body,
        mesh=mesh,
        in_specs=placed,
        out_specs=P(("groups", "store"), None, ("head", "sub")),
        check_vma=False,
    )
```

profile of v0, /device:TPU:0, one launch (start us, length us, event | category | flops | bytes accessed | tf_op | source)
XLA Modules:
  0.0 585.1 jit_solution(8190132482434773607)
XLA Ops:
  9.5 15.8 %all-gather.3.cloned.1.call-done = bf16[8,512,512]{2,1,0:T(8,128)(2,1)} async-done(((bf16[8,256,512]{2,1,0:T(8,128)(2,1)}), bf16[8,512,512]{2,1,0:T(8,128)(2,1)}) %all-gather.3.cloned.1.call-update) | async-done | bytes 4194320 | tf_op jit(solution)/shard_map/all_gather | solution.py:127
  25.3 6.3 %gather_fusion.1 = bf16[12,512,512]{2,1,0:T(8,128)(2,1)} fusion(bf16[8,512,512]{2,1,0:T(8,128)(2,1)} %all-gather.3.cloned.1.call-done, s32[1024]{0:T(1024)S(1)} %pad_clamp_fusion.1), kind=kCustom, calls=%fused_computation.1 | custom fusion | bytes 12582960 | tf_op jit(solution)/shard_map/gather | solution.py:131
  31.7 5.4 all-to-all-start
  40.0 4.9 slice_bitcast_fusion.1
  53.7 3.7 copy.70
  61.1 3.6 copy.40
  65.7 6.3 %gather_fusion.3 = bf16[12,512,512]{2,1,0:T(8,128)(2,1)} fusion(bf16[8,512,512]{2,1,0:T(8,128)(2,1)} %all-gather.5.cloned.1.call-done, s32[1024]{0:T(1024)S(1)} %pad_clamp_fusion.1), kind=kCustom, calls=%fused_computation.3 | custom fusion | bytes 12582960 | tf_op jit(solution)/shard_map/gather | solution.py:132
  72.0 103.9 %all-to-all-done = bf16[4,3,512,512]{3,2,1,0:T(8,128)(2,1)} async-done(((bf16[4,3,512,512]{3,2,1,0:T(8,128)(2,1)}), bf16[4,3,512,512]{3,2,1,0:T(8,128)(2,1)}, u32[]{:S(2)}, u32[]{:S(2)}) %all-to-all-start) | async-done | bytes 6291488 | tf_op jit(solution)/shard_map/all_to_all | solution.py:131
  176.0 5.5 all-to-all-start.1
  181.5 5.8 fusion.26
  187.3 13.6 %fusion.27 = (f32[2,8,528]{2,1,0:T(8,128)S(1)}, f32[2,528,528,8]{2,1,3,0:T(8,128)}) fusion(pred[528,528]{0,1:T(8,128)(4,1)S(1)} %get-tuple-element.238, bf16[528,2,8,128]{3,2,1,0:T(8,128)(2,1)} %bitcast.191, bf16[528,2,128,1]{2,1,0,3:T(2,128)(2,1)S(1)} %bitcast.201), kind=kOutput, calls=%fused_computation.56 | convolution fusion | flops 1155272448 | bytes 20587776 | tf_op jit(solution)/shard_map/rngd,knd->ngrk/dot_general | solution.py:31
  201.7 5.8 fusion.29
  207.6 10.4 %fusion.31 = f32[2,8,528]{2,1,0:T(8,128)S(1)} fusion(f32[2,528,528,8]{2,1,3,0:T(8,128)} %get-tuple-element.235, f32[2,8,528]{2,1,0:T(8,128)S(1)} %broadcast_maximum_fusion, pred[528,528]{0,1:T(8,128)(4,1)S(1)} %get-tuple-element.238), kind=kLoop, calls=%fused_computation.60 | loop fusion | flops 22294272 | bytes 18188544 | tf_op jit(solution)/shard_map/reduce_sum | solution.py:39
  218.0 12.7 %bitcast_add_fusion.3 = f32[528,2,8,128]{3,0,2,1:T(8,128)} fusion(f32[2,528,528,8]{2,1,3,0:T(8,128)} %copy-done.2, f32[2,8,528]{2,1,0:T(8,128)S(1)} %broadcast_maximum_fusion.1, pred[528,528]{0,1:T(8,128)(4,1)S(1)} %get-tuple-element.239, f32[528,2,8]{0,2,1:T(8,128)S(1)} %get-tuple-element.224, bf16[528,2,128,1]{2,1,0,3:T(2,128)(2,1)S(1)} %bitcast.202), kind=kOutput, calls=%fused_computation.67 | convolution fusion | flops 1165283328 | bytes 22784256 | tf_op jit(solution)/shard_map/ngrk,knd->rngd/dot_general | solution.py:41
  230.7 12.7 %bitcast_add_fusion.2 = f32[528,2,8,128]{3,0,2,1:T(8,128)} fusion(f32[2,528,528,8]{2,1,3,0:T(8,128)} %get-tuple-element.235, f32[2,8,528]{2,1,0:T(8,128)S(1)} %broadcast_maximum_fusion, pred[528,528]{0,1:T(8,128)(4,1)S(1)} %get-tuple-element.238, f32[528,2,8]{0,2,1:T(8,128)S(1)} %get-tuple-element.226, bf16[528,2,128,1]{2,1,0,3:T(2,128)(2,1)S(1)} %bitcast.203), kind=kOutput, calls=%fused_computation.66 | convolution fusion | flops 1165283328 | bytes 22784256 | tf_op jit(solution)/shard_map/ngrk,knd->rngd/dot_general | solution.py:41
  243.5 7.0 %gather_fusion.2 = bf16[12,512,512]{2,1,0:T(8,128)(2,1)} fusion(bf16[12,512,512]{2,1,0:T(8,128)(2,1)} %bitcast.31, s32[1024]{0:T(1024)S(1)} %pad_clamp_fusion), kind=kCustom, calls=%fused_computation.2 | custom fusion | bytes 12582960 | tf_op jit(solution)/shard_map/gather | solution.py:134
  250.4 69.1 %all-to-all-done.1 = bf16[4,3,512,512]{3,2,1,0:T(8,128)(2,1)} async-done(((bf16[4,3,512,512]{3,2,1,0:T(8,128)(2,1)}), bf16[4,3,512,512]{3,2,1,0:T(8,128)(2,1)}, u32[]{:S(2)}, u32[]{:S(2)}) %all-to-all-start.1) | async-done | bytes 6291488 | tf_op jit(solution)/shard_map/all_to_all | solution.py:132
  319.6 6.9 %gather_fusion.4 = bf16[12,512,512]{2,1,0:T(8,128)(2,1)} fusion(bf16[12,512,512]{2,1,0:T(8,128)(2,1)} %bitcast.38, s32[1024]{0:T(1024)S(1)} %pad_clamp_fusion), kind=kCustom, calls=%fused_computation.4 | custom fusion | bytes 12582960 | tf_op jit(solution)/shard_map/gather | solution.py:135
  326.5 5.6 constant_dynamic-slice_fusion.6
  332.1 3.5 reshape_squeeze.19
  335.6 3.5 reshape_squeeze.20
  339.1 108.8 %while.28 = (s32[]{:T(128)}, f32[2,8,528]{2,1,0:T(8,128)S(1)}, f32[2,8,528]{2,1,0:T(8,128)S(1)}, f32[528,2,8,128]{3,0,2,1:T(8,128)}, s32[6,512]{1,0:T(8,128)S(1)...) while((s32[]{:T(128)}, f32[2,8,528]{2,1,0:T(8,128)S(1)}, ...), condition=%wide.region_9.10_spmd, body=%wide.region_6.9_spmd.sunk | while | flops 2273551104 | bytes 96200456 | solution.py:61
  349.3 3.0 fusion.87
  352.3 5.6 bitcast_add_fusion.7
  357.9 6.2 %fusion.89 = f32[2,8,528]{2,1,0:T(8,128)S(1)} fusion(f32[2,512,528,8]{1,2,3,0:T(8,128)S(1)} %get-tuple-element.373, f32[2,8,528]{2,1,0:T(8,128)S(1)} %get-tuple-element.448, pred[528,512]{1,0:T(8,128)(4,1)S(1)} %compare_and_fusion.6), kind=kLoop, calls=%fused_computation.11.clone.1 | loop fusion | flops 21618432 | bytes 17639424 | tf_op jit(solution)/shard_map/while/body/eval_jaxpr/reduce_sum | solution.py:39
  366.0 3.0 fusion.87
  369.0 5.6 bitcast_add_fusion.7
  374.6 6.2 %fusion.89 = f32[2,8,528]{2,1,0:T(8,128)S(1)} fusion(f32[2,512,528,8]{1,2,3,0:T(8,128)S(1)} %get-tuple-element.373, f32[2,8,528]{2,1,0:T(8,128)S(1)} %get-tuple-element.448, pred[528,512]{1,0:T(8,128)(4,1)S(1)} %compare_and_fusion.6), kind=kLoop, calls=%fused_computation.11.clone.1 | loop fusion | flops 21618432 | bytes 17639424 | tf_op jit(solution)/shard_map/while/body/eval_jaxpr/reduce_sum | solution.py:39
  382.8 3.0 fusion.87
  385.8 5.6 bitcast_add_fusion.7
  391.4 6.2 %fusion.89 = f32[2,8,528]{2,1,0:T(8,128)S(1)} fusion(f32[2,512,528,8]{1,2,3,0:T(8,128)S(1)} %get-tuple-element.373, f32[2,8,528]{2,1,0:T(8,128)S(1)} %get-tuple-element.448, pred[528,512]{1,0:T(8,128)(4,1)S(1)} %compare_and_fusion.6), kind=kLoop, calls=%fused_computation.11.clone.1 | loop fusion | flops 21618432 | bytes 17639424 | tf_op jit(solution)/shard_map/while/body/eval_jaxpr/reduce_sum | solution.py:39
  399.5 3.0 fusion.87
  402.5 5.6 bitcast_add_fusion.7
  408.1 6.2 %fusion.89 = f32[2,8,528]{2,1,0:T(8,128)S(1)} fusion(f32[2,512,528,8]{1,2,3,0:T(8,128)S(1)} %get-tuple-element.373, f32[2,8,528]{2,1,0:T(8,128)S(1)} %get-tuple-element.448, pred[528,512]{1,0:T(8,128)(4,1)S(1)} %compare_and_fusion.6), kind=kLoop, calls=%fused_computation.11.clone.1 | loop fusion | flops 21618432 | bytes 17639424 | tf_op jit(solution)/shard_map/while/body/eval_jaxpr/reduce_sum | solution.py:39
  416.3 3.0 fusion.87
  419.3 5.6 bitcast_add_fusion.7
  424.9 6.2 %fusion.89 = f32[2,8,528]{2,1,0:T(8,128)S(1)} fusion(f32[2,512,528,8]{1,2,3,0:T(8,128)S(1)} %get-tuple-element.373, f32[2,8,528]{2,1,0:T(8,128)S(1)} %get-tuple-element.448, pred[528,512]{1,0:T(8,128)(4,1)S(1)} %compare_and_fusion.6), kind=kLoop, calls=%fused_computation.11.clone.1 | loop fusion | flops 21618432 | bytes 17639424 | tf_op jit(solution)/shard_map/while/body/eval_jaxpr/reduce_sum | solution.py:39
  433.0 3.0 fusion.87
  436.0 5.6 bitcast_add_fusion.7
  441.6 6.2 %fusion.89 = f32[2,8,528]{2,1,0:T(8,128)S(1)} fusion(f32[2,512,528,8]{1,2,3,0:T(8,128)S(1)} %get-tuple-element.373, f32[2,8,528]{2,1,0:T(8,128)S(1)} %get-tuple-element.448, pred[528,512]{1,0:T(8,128)(4,1)S(1)} %compare_and_fusion.6), kind=kLoop, calls=%fused_computation.11.clone.1 | loop fusion | flops 21618432 | bytes 17639424 | tf_op jit(solution)/shard_map/while/body/eval_jaxpr/reduce_sum | solution.py:39
  447.9 3.1 broadcast_divide_fusion.1
  454.0 3.5 select_convert_fusion.1
  457.6 3.5 reshape_squeeze.22
  461.1 3.5 reshape_squeeze.23
  464.6 100.5 %while.29 = (s32[]{:T(128)}, f32[2,8,528]{2,1,0:T(8,128)S(1)}, f32[2,8,528]{2,1,0:T(8,128)S(1)}, f32[528,2,8,128]{3,0,2,1:T(8,128)}, s32[6,512]{1,0:T(8,128)S(1)...) while((s32[]{:T(128)}, f32[2,8,528]{2,1,0:T(8,128)S(1)}, ...), condition=%wide.region_16.17_spmd, body=%wide.region_13.16_spmd.sunk | while | flops 2273551104 | bytes 96200456 | solution.py:61
  469.5 5.6 bitcast_add_fusion.8
  475.1 6.2 %fusion.94 = f32[2,8,528]{2,1,0:T(8,128)S(1)} fusion(f32[2,512,528,8]{1,2,3,0:T(8,128)S(1)} %get-tuple-element.389, f32[2,8,528]{2,1,0:T(8,128)S(1)} %get-tuple-element.415, pred[528,512]{1,0:T(8,128)(4,1)S(1)} %compare_and_fusion.7), kind=kLoop, calls=%fused_computation.33.clone.1 | loop fusion | flops 21618432 | bytes 17639424 | tf_op jit(solution)/shard_map/while/body/eval_jaxpr/reduce_sum | solution.py:39
  483.2 3.0 fusion.92
  486.2 5.6 bitcast_add_fusion.8
  491.8 6.2 %fusion.94 = f32[2,8,528]{2,1,0:T(8,128)S(1)} fusion(f32[2,512,528,8]{1,2,3,0:T(8,128)S(1)} %get-tuple-element.389, f32[2,8,528]{2,1,0:T(8,128)S(1)} %get-tuple-element.415, pred[528,512]{1,0:T(8,128)(4,1)S(1)} %compare_and_fusion.7), kind=kLoop, calls=%fused_computation.33.clone.1 | loop fusion | flops 21618432 | bytes 17639424 | tf_op jit(solution)/shard_map/while/body/eval_jaxpr/reduce_sum | solution.py:39
  500.0 3.0 fusion.92
  503.0 5.6 bitcast_add_fusion.8
  508.6 6.2 %fusion.94 = f32[2,8,528]{2,1,0:T(8,128)S(1)} fusion(f32[2,512,528,8]{1,2,3,0:T(8,128)S(1)} %get-tuple-element.389, f32[2,8,528]{2,1,0:T(8,128)S(1)} %get-tuple-element.415, pred[528,512]{1,0:T(8,128)(4,1)S(1)} %compare_and_fusion.7), kind=kLoop, calls=%fused_computation.33.clone.1 | loop fusion | flops 21618432 | bytes 17639424 | tf_op jit(solution)/shard_map/while/body/eval_jaxpr/reduce_sum | solution.py:39
  516.7 3.0 fusion.92
  519.7 5.6 bitcast_add_fusion.8
  525.3 6.2 %fusion.94 = f32[2,8,528]{2,1,0:T(8,128)S(1)} fusion(f32[2,512,528,8]{1,2,3,0:T(8,128)S(1)} %get-tuple-element.389, f32[2,8,528]{2,1,0:T(8,128)S(1)} %get-tuple-element.415, pred[528,512]{1,0:T(8,128)(4,1)S(1)} %compare_and_fusion.7), kind=kLoop, calls=%fused_computation.33.clone.1 | loop fusion | flops 21618432 | bytes 17639424 | tf_op jit(solution)/shard_map/while/body/eval_jaxpr/reduce_sum | solution.py:39
  533.5 3.0 fusion.92
  536.5 5.6 bitcast_add_fusion.8
  542.1 6.2 %fusion.94 = f32[2,8,528]{2,1,0:T(8,128)S(1)} fusion(f32[2,512,528,8]{1,2,3,0:T(8,128)S(1)} %get-tuple-element.389, f32[2,8,528]{2,1,0:T(8,128)S(1)} %get-tuple-element.415, pred[528,512]{1,0:T(8,128)(4,1)S(1)} %compare_and_fusion.7), kind=kLoop, calls=%fused_computation.33.clone.1 | loop fusion | flops 21618432 | bytes 17639424 | tf_op jit(solution)/shard_map/while/body/eval_jaxpr/reduce_sum | solution.py:39
  550.2 3.0 fusion.92
  553.2 5.6 bitcast_add_fusion.8
  558.8 6.2 %fusion.94 = f32[2,8,528]{2,1,0:T(8,128)S(1)} fusion(f32[2,512,528,8]{1,2,3,0:T(8,128)S(1)} %get-tuple-element.389, f32[2,8,528]{2,1,0:T(8,128)S(1)} %get-tuple-element.415, pred[528,512]{1,0:T(8,128)(4,1)S(1)} %compare_and_fusion.7), kind=kLoop, calls=%fused_computation.33.clone.1 | loop fusion | flops 21618432 | bytes 17639424 | tf_op jit(solution)/shard_map/while/body/eval_jaxpr/reduce_sum | solution.py:39
  569.9 3.5 reshape.373
  573.8 4.1 pad_maximum_fusion
  (263 shorter events, 52.7 us)
Async XLA Ops:
  6.5 1.5 copy-start
  6.5 18.8 %all-gather.3.cloned.1.call-start = ((), (), s32[]{:S(2)}) async-start(), calls=%async_computation.2 | async-start | bytes 6291456 | tf_op jit(solution)/shard_map/all_gather | solution.py:127
  31.7 6.2 %copy-start.8 = (bf16[2,528,512]{2,1,0:T(8,128)(2,1)S(1)}, bf16[2,528,512]{2,1,0:T(8,128)(2,1)}, u32[]{:S(2)}) copy-start(bf16[2,528,512]{2,1,0:T(8,128)(2,1)} %param.14) | copy-start | bytes 3244036
  31.7 6.4 %copy-start.19 = (s32[8]{0:T(128)S(1)}, s32[8]{0:T(128)}, u32[]{:S(2)}) copy-start(s32[8]{0:T(128)} %param.21) | copy-start | bytes 100
  31.7 144.3 %all-to-all-start = ((bf16[4,3,512,512]{3,2,1,0:T(8,128)(2,1)}), bf16[4,3,512,512]{3,2,1,0:T(8,128)(2,1)}, u32[]{:S(2)}, u32[]{:S(2)}) async-start(bf16[4,3,512,512]{3,2,1,0:T(8,128)(2,1)} %bitcast.186), calls=%async_computation | async-start | bytes 12582912 | tf_op jit(solution)/shard_map/all_to_all | solution.py:131
  37.0 28.6 %all-gather.5.cloned.1.call-start = ((), (), s32[]{:S(2)}) async-start(), calls=%async_computation.3 | async-start | bytes 6291456 | tf_op jit(solution)/shard_map/all_gather | solution.py:128
  40.0 6.9 %copy-start.9 = (bf16[2,528,512]{2,1,0:T(8,128)(2,1)S(1)}, bf16[2,528,512]{2,1,0:T(8,128)(2,1)}, u32[]{:S(2)}) copy-start(bf16[2,528,512]{2,1,0:T(8,128)(2,1)} %param.15) | copy-start | bytes 3244036
  64.6 7.4 %copy-start.15 = (pred[528]{0:T(1024)(128)(4,1)}, pred[528]{0:T(1024)(128)(4,1)S(1)}, u32[]{:S(2)}) copy-start(pred[528]{0:T(1024)(128)(4,1)S(1)} %iota_compare_fusion.2) | copy-start | bytes 1588
  64.7 7.4 %copy-start.17 = (pred[528]{0:T(1024)(128)(4,1)}, pred[528]{0:T(1024)(128)(4,1)S(1)}, u32[]{:S(2)}) copy-start(pred[528]{0:T(1024)(128)(4,1)S(1)} %iota_compare_fusion.3) | copy-start | bytes 1588
  65.0 7.1 %copy-start.12 = (s32[528]{0:T(1024)}, s32[528]{0:T(1024)S(1)}, u32[]{:S(2)}) copy-start(s32[528]{0:T(1024)S(1)} %get-tuple-element.397) | copy-start | bytes 6340
  176.0 143.6 %all-to-all-start.1 = ((bf16[4,3,512,512]{3,2,1,0:T(8,128)(2,1)}), bf16[4,3,512,512]{3,2,1,0:T(8,128)(2,1)}, u32[]{:S(2)}, u32[]{:S(2)}) async-start(bf16[4,3,512,512]{3,2,1,0:T(8,128)(2,1)} %bitcast.187), calls=%async_computation.1 | async-start | bytes 12582912 | tf_op jit(solution)/shard_map/all_to_all | solution.py:132
  187.3 14.4 %copy-start.2 = (f32[2,528,528,8]{2,1,3,0:T(8,128)}, f32[2,528,528,8]{2,1,3,0:T(8,128)S(1)}, u32[]{:S(2)}) copy-start(f32[2,528,528,8]{2,1,3,0:T(8,128)S(1)} %get-tuple-element.237) | copy-start | bytes 53526532
  200.9 29.8 %copy-start.4 = (f32[2,8,528]{2,1,0:T(8,128)}, f32[2,8,528]{2,1,0:T(8,128)S(1)}, u32[]{:S(2)}) copy-start(f32[2,8,528]{2,1,0:T(8,128)S(1)} %broadcast_maximum_fusion) | copy-start | bytes 101380
  207.6 10.4 %copy-start.10 = (bf16[528,2,128]{2,1,0:T(2,128)(2,1)S(1)}, bf16[528,2,128]{2,1,0:T(2,128)(2,1)}, u32[]{:S(2)}) copy-start(bf16[528,2,128]{2,1,0:T(2,128)(2,1)} %reshape.359) | copy-start | bytes 811012
  218.0 12.8 %copy-start.11 = (bf16[528,2,128]{2,1,0:T(2,128)(2,1)S(1)}, bf16[528,2,128]{2,1,0:T(2,128)(2,1)}, u32[]{:S(2)}) copy-start(bf16[528,2,128]{2,1,0:T(2,128)(2,1)} %reshape.371) | copy-start | bytes 811012
  347.7 4.6 slice-start.2
  349.3 3.0 slice-start.3
  357.9 6.2 %copy-start.7 = (f32[528,2,8,128]{3,0,2,1:T(8,128)}, f32[528,2,8,128]{3,0,2,1:T(8,128)S(1)}, u32[]{:S(2)}) copy-start(f32[528,2,8,128]{3,0,2,1:T(8,128)S(1)} %bitcast_add_fusion.7) | copy-start | bytes 12976132 | tf_op jit(solution)/shard_map/while
  364.4 4.6 slice-start.2
  366.0 3.0 slice-start.3
  374.6 6.2 %copy-start.7 = (f32[528,2,8,128]{3,0,2,1:T(8,128)}, f32[528,2,8,128]{3,0,2,1:T(8,128)S(1)}, u32[]{:S(2)}) copy-start(f32[528,2,8,128]{3,0,2,1:T(8,128)S(1)} %bitcast_add_fusion.7) | copy-start | bytes 12976132 | tf_op jit(solution)/shard_map/while
  381.2 4.6 slice-start.2
  382.8 3.0 slice-start.3
  391.4 6.2 %copy-start.7 = (f32[528,2,8,128]{3,0,2,1:T(8,128)}, f32[528,2,8,128]{3,0,2,1:T(8,128)S(1)}, u32[]{:S(2)}) copy-start(f32[528,2,8,128]{3,0,2,1:T(8,128)S(1)} %bitcast_add_fusion.7) | copy-start | bytes 12976132 | tf_op jit(solution)/shard_map/while
  397.9 4.6 slice-start.2
  399.5 3.0 slice-start.3
  408.1 6.2 %copy-start.7 = (f32[528,2,8,128]{3,0,2,1:T(8,128)}, f32[528,2,8,128]{3,0,2,1:T(8,128)S(1)}, u32[]{:S(2)}) copy-start(f32[528,2,8,128]{3,0,2,1:T(8,128)S(1)} %bitcast_add_fusion.7) | copy-start | bytes 12976132 | tf_op jit(solution)/shard_map/while
  414.7 4.6 slice-start.2
  416.3 3.0 slice-start.3
  424.9 6.2 %copy-start.7 = (f32[528,2,8,128]{3,0,2,1:T(8,128)}, f32[528,2,8,128]{3,0,2,1:T(8,128)S(1)}, u32[]{:S(2)}) copy-start(f32[528,2,8,128]{3,0,2,1:T(8,128)S(1)} %bitcast_add_fusion.7) | copy-start | bytes 12976132 | tf_op jit(solution)/shard_map/while
  431.4 4.6 slice-start.2
  433.0 3.0 slice-start.3
  441.6 6.2 %copy-start.7 = (f32[528,2,8,128]{3,0,2,1:T(8,128)}, f32[528,2,8,128]{3,0,2,1:T(8,128)S(1)}, u32[]{:S(2)}) copy-start(f32[528,2,8,128]{3,0,2,1:T(8,128)S(1)} %bitcast_add_fusion.7) | copy-start | bytes 12976132 | tf_op jit(solution)/shard_map/while
  447.9 6.1 %copy-start.18 = (pred[528]{0:T(1024)(128)(4,1)S(1)}, pred[528]{0:T(1024)(128)(4,1)}, u32[]{:S(2)}) copy-start(pred[528]{0:T(1024)(128)(4,1)} %copy-done.17) | copy-start | bytes 1588
  454.0 10.5 %copy-start.3 = (bf16[528,2,8,128]{3,0,2,1:T(8,128)(2,1)S(1)}, bf16[528,2,8,128]{3,0,2,1:T(8,128)(2,1)}, u32[]{:S(2)}) copy-start(bf16[528,2,8,128]{3,0,2,1:T(8,128)(2,1)} %copy.40) | copy-start | bytes 6488068
  454.0 10.5 %copy-start.5 = (f32[2,8,528]{2,1,0:T(8,128)S(1)}, f32[2,8,528]{2,1,0:T(8,128)}, u32[]{:S(2)}) copy-start(f32[2,8,528]{2,1,0:T(8,128)} %copy-done.4) | copy-start | bytes 101380
  454.0 10.5 %copy-start.13 = (s32[528]{0:T(1024)S(1)}, s32[528]{0:T(1024)}, u32[]{:S(2)}) copy-start(s32[528]{0:T(1024)} %copy-done.12) | copy-start | bytes 6340
  454.0 10.5 %copy-start.14 = (pred[6,512]{1,0:T(8,128)(4,1)S(1)}, pred[6,512]{1,0:T(8,128)(4,1)}, u32[]{:S(2)}) copy-start(pred[6,512]{1,0:T(8,128)(4,1)} %reshape.372) | copy-start | bytes 9220
  464.9 4.6 slice-start
  466.4 3.0 slice-start.1
  475.0 6.2 %copy-start.6 = (f32[528,2,8,128]{3,0,2,1:T(8,128)}, f32[528,2,8,128]{3,0,2,1:T(8,128)S(1)}, u32[]{:S(2)}) copy-start(f32[528,2,8,128]{3,0,2,1:T(8,128)S(1)} %bitcast_add_fusion.8) | copy-start | bytes 12976132 | tf_op jit(solution)/shard_map/while
  481.6 4.6 slice-start
  483.2 3.0 slice-start.1
  491.8 6.2 %copy-start.6 = (f32[528,2,8,128]{3,0,2,1:T(8,128)}, f32[528,2,8,128]{3,0,2,1:T(8,128)S(1)}, u32[]{:S(2)}) copy-start(f32[528,2,8,128]{3,0,2,1:T(8,128)S(1)} %bitcast_add_fusion.8) | copy-start | bytes 12976132 | tf_op jit(solution)/shard_map/while
  498.4 4.6 slice-start
  499.9 3.0 slice-start.1
  508.5 6.2 %copy-start.6 = (f32[528,2,8,128]{3,0,2,1:T(8,128)}, f32[528,2,8,128]{3,0,2,1:T(8,128)S(1)}, u32[]{:S(2)}) copy-start(f32[528,2,8,128]{3,0,2,1:T(8,128)S(1)} %bitcast_add_fusion.8) | copy-start | bytes 12976132 | tf_op jit(solution)/shard_map/while
  515.1 4.6 slice-start
  516.7 3.0 slice-start.1
  525.3 6.2 %copy-start.6 = (f32[528,2,8,128]{3,0,2,1:T(8,128)}, f32[528,2,8,128]{3,0,2,1:T(8,128)S(1)}, u32[]{:S(2)}) copy-start(f32[528,2,8,128]{3,0,2,1:T(8,128)S(1)} %bitcast_add_fusion.8) | copy-start | bytes 12976132 | tf_op jit(solution)/shard_map/while
  531.9 4.6 slice-start
  533.4 3.0 slice-start.1
  542.1 6.2 %copy-start.6 = (f32[528,2,8,128]{3,0,2,1:T(8,128)}, f32[528,2,8,128]{3,0,2,1:T(8,128)S(1)}, u32[]{:S(2)}) copy-start(f32[528,2,8,128]{3,0,2,1:T(8,128)S(1)} %bitcast_add_fusion.8) | copy-start | bytes 12976132 | tf_op jit(solution)/shard_map/while
  548.6 4.6 slice-start
  550.2 3.0 slice-start.1
  558.8 6.2 %copy-start.6 = (f32[528,2,8,128]{3,0,2,1:T(8,128)}, f32[528,2,8,128]{3,0,2,1:T(8,128)S(1)}, u32[]{:S(2)}) copy-start(f32[528,2,8,128]{3,0,2,1:T(8,128)S(1)} %bitcast_add_fusion.8) | copy-start | bytes 12976132 | tf_op jit(solution)/shard_map/while
  565.1 8.3 %copy-start.16 = (pred[528]{0:T(1024)(128)(4,1)S(1)}, pred[528]{0:T(1024)(128)(4,1)}, u32[]{:S(2)}) copy-start(pred[528]{0:T(1024)(128)(4,1)} %copy-done.15) | copy-start | bytes 1588
  569.9 8.0 %copy-start.1 = (s32[32]{0:T(128)S(1)}, s32[32]{0:T(128)}, u32[]{:S(2)}) copy-start(s32[32]{0:T(128)} %param.19) | copy-start | bytes 388
Sparse Core Ops, SparseCore 0:
  8.9 16.3 all-gather.2
  39.4 15.2 all-gather.4
where the time goes:
time: 594 us; the launch traced here: 585 us
  waiting for transfers between devices  190 us (32%)
  matrix products  147 us (25%)
  other arithmetic  111 us (19%)
  local copies, waits for them, and re-layouts  100 us (17%)
  between operations  15.5 us (3%)
  starting transfers between devices  10.9 us (2%)
  loops' own time  9.74 us (2%)
    all_to_all x1, waiting for transfers between devices, body(): lax.all_to_all(whole_keys[send_place], 'store', split_axis=0, concat_axis...  104 us
    dot_general x14, matrix products, attend_block(): jnp.einsum('ngrk,knd->rngd', weights, block_values, preferred_element_typ...  92.4 us
    reduce_sum x14, other arithmetic, attend_block(): totals = totals * factor + jnp.sum(powers, axis=-1)  90.6 us
    all_to_all x1, waiting for transfers between devices, body(): lax.all_to_all(whole_values[send_place], 'store', split_axis=0, concat_ax...  69.1 us
    dot_general x14, matrix products, attend_block(): jnp.einsum('rngd,knd->ngrk', query_four, block_keys, preferred_element_ty...  54.9 us
    dynamic_slice x36, local copies, waits for them, and re-layouts, context_pass(): lax.scan(advance, carried, (block_keys, block_values, block_pos, block_li...  19 us
    all_gather x1, waiting for transfers between devices, body(): lax.all_gather(store_keys, 'sub', axis=1, tiled=True)  15.8 us
  transfers between devices with their start and end apart: 4, of which 3 were waited for; matrix products, arithmetic and copies ran while one was open for 18% of the time, Pallas kernels for 0%

commit v1 on v0

v1 whole, which is shorter than its diff:
```python
import functools
import math

import jax
import jax.numpy as jnp
from jax import lax
from jax.experimental import pallas as pl
from jax.experimental.pallas import tpu as pltpu
from jax.sharding import PartitionSpec as P

HD = 128
GROUP = 8
NEGATIVE = -1e30
FAR = 1 << 20
CHAIN = 2
VMEM_BYTES = 52 * 1024 * 1024


def row_tile(rows):
    for size in range(192, 15, -16):
        if rows % size == 0:
            return size
    return rows


def round_up(value, unit):
    return (value + unit - 1) // unit * unit


def pack_kernel(stores, capacity, req_dev, nch, ch_dev, q_heads, kv_used, ids, slots, keys, values, *rest):
    outs = rest[: 2 * stores]
    sems = rest[2 * stores]
    me = lax.axis_index("store")
    core = lax.axis_index("sub")
    width = kv_used * HD

    def copies(d, e, place, rank):
        column = pl.multiple_of(lax.rem(core + e, 2) * q_heads // GROUP * HD, HD)
        return [
            pltpu.make_async_copy(
                source.at[place, :, pl.ds(column, width)],
                outs[2 * d + e].at[rank, which],
                sems.at[((d * capacity + rank) * 2 + e) * 2 + which],
            )
            for which, source in enumerate((keys, values))
        ]

    counts = []
    for step in range(stores):
        d = (step + 1) % stores
        target = lax.rem(me + d, stores)

        def visit(j, rank):
            request = target * req_dev + lax.div(j, nch)
            slot = slots[ids[request, lax.rem(j, nch)]]
            place = lax.rem(slot, ch_dev)
            hit = lax.div(slot, ch_dev) == me

            @pl.when(hit)
            def _():
                for e in range(2):
                    for copy in copies(d, e, place, rank):
                        copy.start()

            return rank + hit.astype(jnp.int32)

        counts.append((d, lax.fori_loop(0, req_dev * nch, visit, jnp.int32(0))))
    for d, count in counts:

        def finish(rank, unused):
            for e in range(2):
                for copy in copies(d, e, 0, rank):
                    copy.wait()
            return unused

        lax.fori_loop(0, count, finish, 0)


def attend_kernel(offsets, first, last, per_kv, nch, select, rows, tile, half, *refs):
    table, lens, column, q_ref, kf_ref, vf_ref, qpos_ref, kpos_ref = refs[:8]
    pieces = refs[8 : 8 + 2 * len(offsets)]
    rest = list(refs[8 + 2 * len(offsets) :])
    if not first:
        acc_in, ml_in = rest[:2]
        rest = rest[2:]
    if last:
        out_ref = rest[0]
        rest = rest[1:]
    else:
        acc_out, ml_out = rest[:2]
        rest = rest[2:]
    acc_ref, m_ref, k_scr, v_scr, page_v = rest
    request = pl.program_id(0)
    scale = HD ** (-0.5) * math.log2(math.e)
    chain = min(CHAIN, per_kv)
    tiles = rows // tile
    lens_here = lens[request]

    def wide(value, width):
        return jnp.concatenate([value] * (width // HD), axis=1)

    def attend(spot, row_at, keys, values, biases, begin):
        heads = pl.ds(spot * chain, chain)
        span = pl.ds(row_at, tile)
        q = jnp.concatenate(
            [q_ref[0, span, (spot * chain + h) * HD : (spot * chain + h + 1) * HD] for h in range(chain)], axis=0
        )
        scores = []
        for k, bias in zip(keys, biases):
            s = lax.dot_general(q, k, (((1,), (1,)), ((), ())), preferred_element_type=jnp.float32)
            s = s.reshape(chain, tile, s.shape[1]) + bias[None]
            scores.append(s.reshape(chain * tile, s.shape[2]))
        peak = jnp.max(scores[0], axis=-1, keepdims=True)
        for s in scores[1:]:
            peak = jnp.maximum(peak, jnp.max(s, axis=-1, keepdims=True))
        if begin:
            m_new = jnp.broadcast_to(peak, (chain * tile, HD))
        else:
            m_old = m_ref[heads, span, :].reshape(chain * tile, HD)
            m_new = jnp.maximum(m_old, peak)
        update = None
        for s, v in zip(scores, values):
            p = jnp.exp2((s - wide(m_new, s.shape[1])) * scale).astype(jnp.bfloat16)
            part = jnp.dot(p, v, preferred_element_type=jnp.float32)
            update = part if update is None else update + part
        if not begin:
            factor = jnp.exp2((m_old - m_new) * scale)
            update = acc_ref[heads, span, :].reshape(chain * tile, 2 * HD) * wide(factor, 2 * HD) + update
        acc_ref[heads, span, :] = update.reshape(chain, tile, 2 * HD)
        m_ref[heads, span, :] = m_new.reshape(chain, tile, HD)

    page_v[:, :, HD:] = jnp.ones((2, half, HD), jnp.bfloat16)
    if first:
        padded = k_scr.shape[0]
        k_scr[...] = jnp.zeros(k_scr.shape, jnp.bfloat16)
        v_scr[:, :HD] = jnp.zeros((padded, HD), jnp.bfloat16)
        v_scr[:, HD:] = jnp.ones((padded, HD), jnp.bfloat16)
        k_scr[:rows, :] = kf_ref[0]
        v_scr[:rows, :HD] = vf_ref[0]
        for t in range(tiles):
            end = min(round_up((t + 1) * tile, HD), padded)
            row_id = lax.broadcasted_iota(jnp.int32, (tile, end), 0) + t * tile
            key_id = lax.broadcasted_iota(jnp.int32, (tile, end), 1)
            allowed = (key_id <= row_id) & (key_id < select + lens_here)
            bias = jnp.where(allowed, 0.0, NEGATIVE)
            for spot in range(per_kv // chain):
                attend(spot, t * tile, [k_scr[:end, :]], [v_scr[:end, :]], [bias], True)
    else:
        ml = ml_in[0]
        acc_ref[:, :, :HD] = acc_in[0]
        m_ref[...] = jnp.broadcast_to(ml[:, :, :1], ml.shape)
        acc_ref[:, :, HD:] = jnp.broadcast_to(ml[:, :, HD // 2 : HD // 2 + 1], ml.shape)

    core = lax.axis_index("sub")

    def page(chunk, unused):
        base = (request * nch + chunk) * 3
        offset, rank, tile_from = table[base], table[base + 1], table[base + 2]
        for at, d in enumerate(offsets):

            @pl.when(offset == d)
            def _():
                keys = [pieces[2 * at + e][rank, 0] for e in range(2)]
                for e in range(2):
                    page_v[e, :, :HD] = pieces[2 * at + e][rank, 1]
                kpos = [kpos_ref[0, chunk * 2 + lax.rem(core + e, 2)] for e in range(2)]

                def one_tile(t, unused):
                    row_at = pl.multiple_of(t * tile, 16)
                    qpos = qpos_ref[0, pl.ds(row_at, tile), :]
                    biases = [jnp.where(kp <= qpos, 0.0, NEGATIVE) for kp in kpos]
                    for spot in range(per_kv // chain):
                        attend(spot, row_at, keys, [page_v[e] for e in range(2)], biases, False)
                    return unused

                lax.fori_loop(tile_from, tiles, one_tile, 0)

        return unused

    lax.fori_loop(0, nch, page, 0)

    if last:
        live = lax.broadcasted_iota(jnp.int32, (rows, HD), 0) < select + lens_here
        for h in range(per_kv):
            result = acc_ref[h, :, :HD] / acc_ref[h, :, HD:]
            out_ref[0, :, h * HD : (h + 1) * HD] = jnp.where(live, result, 0.0).astype(jnp.bfloat16)
    else:
        lane = lax.broadcasted_iota(jnp.int32, m_ref.shape, 2)
        acc_out[0] = acc_ref[:, :, :HD]
        ml_out[0] = jnp.where(lane < HD // 2, m_ref[...], acc_ref[:, :, HD:])


def body(groups_of, fresh_query, fresh_keys, fresh_values, store_keys, store_values, span_ids, span_slot, select_pos, ask_len):
    stores = lax.axis_size("store")
    store_index = lax.axis_index("store")
    core = lax.axis_index("sub")
    req_dev, rows, q_columns = fresh_query.shape
    ch_dev, half, unused = store_keys.shape
    nch = span_ids.shape[1]
    select = select_pos.shape[1]
    span = 2 * half
    context = nch * span
    references = req_dev * nch
    capacity = (references + stores - 1) // stores
    q_heads = q_columns // HD
    kv_used = max(q_heads // GROUP, 1)
    per_kv = q_heads // kv_used
    tile = row_tile(rows)

    piece = jax.ShapeDtypeStruct((capacity, 2, half, kv_used * HD), jnp.bfloat16)
    smem = pl.BlockSpec(memory_space=pltpu.SMEM)
    anywhere = pl.BlockSpec(memory_space=pl.ANY)
    packed = pl.pallas_call(
        functools.partial(pack_kernel, stores, capacity, req_dev, nch, ch_dev, q_heads, kv_used),
        out_shape=[piece] * (2 * stores),
        in_specs=[smem, smem, anywhere, anywhere],
        out_specs=[anywhere] * (2 * stores),
        scratch_shapes=[pltpu.SemaphoreType.DMA((stores * capacity * 4,))],
        name="pack_spans",
    )(span_ids, span_slot, store_keys, store_values)

    pieces = {}
    for group in groups_of(stores):
        for d in group:
            for e in range(2):
                block = packed[2 * d + e]
                if (d, e) != (0, 0):
                    pairs = [
                        (s * 2 + c, ((s + d) % stores) * 2 + (c + e) % 2) for s in range(stores) for c in range(2)
                    ]
                    block = lax.ppermute(block, ("store", "sub"), pairs)
                pieces[(d, e)] = block

    my_pos = lax.dynamic_slice_in_dim(select_pos, store_index * req_dev, req_dev, 0)
    my_len = lax.dynamic_slice_in_dim(ask_len, store_index * req_dev, req_dev, 0)
    my_ids = lax.dynamic_slice_in_dim(span_ids, store_index * req_dev, req_dev, 0).reshape(references)
    my_owners = span_slot[my_ids] // ch_dev
    earlier = jnp.arange(references)[None, :] < jnp.arange(references)[:, None]
    my_ranks = jnp.sum((my_owners[:, None] == my_owners[None, :]) & earlier, axis=1, dtype=jnp.int32)
    my_offsets = (store_index - my_owners + stores) % stores
    chunk_at = jnp.arange(nch, dtype=jnp.int32) * span
    before = jnp.sum(my_pos[:, None, :] < chunk_at[None, :, None], axis=2, dtype=jnp.int32).reshape(references)
    table = jnp.stack([my_offsets, my_ranks, before // tile], axis=1).astype(jnp.int32).reshape(references * 3)
    places = jnp.arange(context, dtype=jnp.int32)
    chosen = jnp.any(my_pos[:, :, None] == places[None, None, :], axis=1)
    key_pos = jnp.where(chosen, FAR, places[None, :]).reshape(req_dev, nch * 2, 1, half)
    tail = jnp.broadcast_to(context + jnp.arange(rows - select, dtype=jnp.int32), (req_dev, rows - select))
    query_pos = jnp.concatenate([my_pos, tail], axis=1)[:, :, None]
    column = (core * q_heads // GROUP).astype(jnp.int32).reshape(1)

    state_block = pl.BlockSpec((1, per_kv, rows, HD), lambda r, n, *s: (r * kv_used + n, 0, 0, 0))
    state_shape = jax.ShapeDtypeStruct((req_dev * kv_used, per_kv, rows, HD), jnp.float32)
    head_block = pl.BlockSpec((1, rows, per_kv * HD), lambda r, n, *s: (r, 0, n))
    fresh_block = pl.BlockSpec((1, rows, HD), lambda r, n, t, l, c: (r, 0, c[0] + n))
    state = []
    steps = groups_of(stores)
    padded = round_up(rows, HD)
    for at, group in enumerate(steps):
        first, last = at == 0, at == len(steps) - 1
        blocks = [pieces[(d, e)] for d in group for e in range(2)]
        in_specs = [
            head_block,
            fresh_block,
            fresh_block,
            pl.BlockSpec((1, rows, 1), lambda r, n, *s: (r, 0, 0)),
            pl.BlockSpec((1, nch * 2, 1, half), lambda r, n, *s: (r, 0, 0, 0)),
        ]
        in_specs += [pl.BlockSpec((capacity, 2, half, HD), lambda r, n, *s: (0, 0, 0, n))] * len(blocks)
        in_specs += [state_block] * len(state)
        flops = 4 * req_dev * q_heads * rows * HD * (context * len(group) // stores // 2 + (rows // 2 if first else 0))
        state = pl.pallas_call(
            functools.partial(
                attend_kernel, tuple(group), first, last, per_kv, nch, select, rows, tile, half
            ),
            grid_spec=pltpu.PrefetchScalarGridSpec(
                num_scalar_prefetch=3,
                grid=(req_dev, kv_used),
                in_specs=in_specs,
                out_specs=[head_block] if last else [state_block] * 2,
                scratch_shapes=[
                    pltpu.VMEM((per_kv, rows, 2 * HD), jnp.float32),
                    pltpu.VMEM((per_kv, rows, HD), jnp.float32),
                    pltpu.VMEM((padded, HD), jnp.bfloat16),
                    pltpu.VMEM((padded, 2 * HD), jnp.bfloat16),
                    pltpu.VMEM((2, half, 2 * HD), jnp.bfloat16),
                ],
            ),
            out_shape=[jax.ShapeDtypeStruct(fresh_query.shape, jnp.bfloat16)] if last else [state_shape] * 2,
            compiler_params=pltpu.CompilerParams(vmem_limit_bytes=VMEM_BYTES),
            cost_estimate=pl.CostEstimate(flops=flops, bytes_accessed=30 << 20, transcendentals=flops // (4 * HD)),
            name="attend_pages",
        )(table, my_len, column, fresh_query, fresh_keys, fresh_values, query_pos, key_pos, *blocks, *state)
    return state[0]


def groups_of(stores):
    near = [d for d in range(1, stores) if min(d, stores - d) <= stores // 4]
    far = [d for d in range(1, stores) if d not in near]
    return [group for group in ([0], near, far) if group]


def solution(mesh):
    placed = (
        P(("groups", "store"), None, ("head", "sub")),
        P(("groups", "store"), None, "head"),
        P(("groups", "store"), None, "head"),
        P(("groups", "store"), "sub", "head"),
        P(("groups", "store"), "sub", "head"),
        P("groups", None),
        P("groups"),
        P("groups", None),
        P("groups"),
    )
    return jax.shard_map(
        functools.partial(body, groups_of),
        mesh=mesh,
        in_specs=placed,
        out_specs=P(("groups", "store"), None, ("head", "sub")),
        check_vma=False,
    )
```

time: 594 us -> 385 us (0.65)
  the two profiles are of different devices: /device:TPU:0 before, /device:TPU:19 now
where the time goes in v1:
time: 385 us
  Pallas kernels  314 us (82%)
  waiting for transfers between devices  53.5 us (14%)
  starting transfers between devices  9.44 us (2%)
  local copies, waits for them, and re-layouts  5.61 us (1%)
    pallas_call x1, Pallas kernels, body(): pl.pallas_call(functools.partial(pack_kernel, stores, capacity, req_dev,...  193 us
    pallas_call x3, Pallas kernels, body(): pl.pallas_call(functools.partial(attend_kernel, tuple(group), first, last...  121 us
    ppermute x7, waiting for transfers between devices, body(): block = lax.ppermute(block, ('store', 'sub'), pairs)  53.5 us
    ppermute x7, starting transfers between devices, body(): block = lax.ppermute(block, ('store', 'sub'), pairs)  9.44 us
  transfers between devices with their start and end apart: 7, of which 2 were waited for; matrix products, arithmetic and copies ran while one was open for 1% of the time, Pallas kernels for 23%

profile of v1, /device:TPU:19, one launch (start us, length us, event | category | flops | bytes accessed | tf_op | source)
XLA Modules:
  0.0 384.7 jit_solution(1076494334137405966)
XLA Ops:
  0.0 0.0 copy-start
  0.0 0.0 copy-start.2
  0.0 0.0 copy-start.6
  0.0 193.1 %pack_spans.1 = (bf16[3,2,256,256]{3,2,1,0:T(8,128)(2,1)}, bf16[3,2,256,256]{3,2,1,0:T(8,128)(2,1)}, bf16[3,2,256,256]{3,2,1,0:T(8,128)(2,1)}, bf16[3,2,256,256]...) custom-call(s32[8,6]{1,0:T(8,128)} %ids.1, ...), custom_call_target="tpu_custom_call" | custom-call | tf_op jit(solution)/shard_map/pack_spans/pallas_call | solution.py:213
  193.1 1.4 collective-permute-start.2
  194.5 0.7 collective-permute-start.3
  195.2 1.6 collective-permute-start.4
  196.8 0.0 collective-permute-start.5
  196.8 0.5 collective-permute-start.6
  197.3 0.7 constant_dynamic-slice_fusion.1
  198.0 0.0 copy-done
  198.0 0.2 fusion.1
  198.3 0.1 reshape.226
  198.4 0.1 copy.16
  198.5 0.1 and.81
  198.6 0.1 copy.17
  198.7 0.1 div.51
  198.8 0.0 copy-done.2
  198.8 0.7 gather_fusion
  199.5 0.2 convert_reduce_fusion
  199.7 0.1 pad.1.clone
  199.8 1.6 fusion
  201.4 0.0 copy-done.6
  201.4 0.1 dynamic_slice.11.refs_1_
  201.5 0.1 copy.18
  201.6 0.1 reshape.227.refs_0_
  201.7 0.2 copy.22.refs_6_
  202.0 9.8 %collective-permute-done.2.refs_8_ = bf16[3,2,256,256]{3,2,1,0:T(8,128)(2,1)S(1)} collective-permute-done((bf16[3,2,256,256]{3,2,1,0:T(8,128)(2,1)}, bf16[3,2,256,256]{3,2,1,0:T(8,128)(2,1)S(1)}, u32[]{:S(2)}, u32[]{:S(2)}) %collective-permute-start.2) | collective-permute-done | bytes 786464 | tf_op jit(solution)/shard_map/ppermute | solution.py:231
  211.8 2.1 collective-permute-start
  213.9 0.0 collective-permute-done.6.refs_9_
  213.9 3.1 collective-permute-start.1
  217.0 0.0 copy-start.1
  217.0 1.1 copy-done.1
  218.1 36.2 %attend_pages.3 = (f32[4,8,528,128]{3,2,1,0:T(8,128)}, f32[4,8,528,128]{3,2,1,0:T(8,128)}) custom-call(s32[36]{0:T(128)S(1)} %reshape.227.refs_0_, s32[2]{0:T(128)S(1)} %dynamic_slice.11.refs_1_, s32[1]{0:T(128)} %bitcast.3.refs_2_, bf16[2,528,2048]{2,1,0:T(8,128)(2,1)} %refs_3_.5, bf16[2,528,512]{2,1,0:T(8,128)(2,1)} %refs_4_.5, ...), custom_call_target="tpu_custom_call" | custom-call | flops 5605687296 | bytes 31457280 | tf_op jit(solution)/shard_map/attend_pages/pallas_call | solution.py:271
  254.3 43.7 %collective-permute-done.3.refs_9_ = bf16[3,2,256,256]{3,2,1,0:T(8,128)(2,1)S(1)} collective-permute-done((bf16[3,2,256,256]{3,2,1,0:T(8,128)(2,1)}, bf16[3,2,256,256]{3,2,1,0:T(8,128)(2,1)S(1)}, u32[]{:S(2)}, u32[]{:S(2)}) %collective-permute-start.3) | collective-permute-done | bytes 786464 | tf_op jit(solution)/shard_map/ppermute | solution.py:231
  298.0 0.0 copy-start.3
  298.0 0.0 collective-permute-done.4.refs_10_
  298.0 0.0 copy-start.4
  298.1 0.0 collective-permute-done.5.refs_11_
  298.1 0.9 copy-done.3
  298.9 0.3 copy-done.4
  299.2 51.0 %attend_pages.4 = (f32[4,8,528,128]{3,2,1,0:T(8,128)}, f32[4,8,528,128]{3,2,1,0:T(8,128)}) custom-call(s32[36]{0:T(128)S(1)} %reshape.227.refs_0_, s32[2]{0:T(128)S(1)} %dynamic_slice.11.refs_1_, s32[1]{0:T(128)} %bitcast.3.refs_2_, bf16[2,528,2048]{2,1,0:T(8,128)(2,1)} %refs_3_.5, bf16[2,528,512]{2,1,0:T(8,128)(2,1)} %refs_4_.5, ...), custom_call_target="tpu_custom_call" | custom-call | flops 6643777536 | bytes 31457280 | tf_op jit(solution)/shard_map/attend_pages/pallas_call | solution.py:271
  350.2 0.0 collective-permute-done.refs_8_
  350.2 0.0 collective-permute-done.1.refs_9_
  350.2 0.0 copy-start.5
  350.2 0.9 copy-done.5
  351.1 33.6 %attend_pages.5 = bf16[2,528,2048]{2,1,0:T(8,128)(2,1)} custom-call(s32[36]{0:T(128)S(1)} %reshape.227.refs_0_, s32[2]{0:T(128)S(1)} %dynamic_slice.11.refs_1_, s32[1]{0:T(128)} %bitcast.3.refs_2_, bf16[2,528,2048]{2,1,0:T(8,128)(2,1)} %refs_3_.5, bf16[2,528,512]{2,1,0:T(8,128)(2,1)} %refs_4_.5, bf16[2,528,512]{2,1,0:T(8,128)(2,1)} %refs_5_.5, ...), custom_call_target="tpu_custom_call" | custom-call | flops 3321888768 | bytes 31457280 | tf_op jit(solution)/shard_map/attend_pages/pallas_call | solution.py:271
  (15 shorter events, 0.2 us)
Async XLA Ops:
  0.0 198.0 %copy-start = (s32[8,464]{1,0:T(8,128)S(1)}, s32[8,464]{1,0:T(8,128)}, u32[]{:S(2)}) copy-start(s32[8,464]{1,0:T(8,128)} %param.16) | copy-start | bytes 44548
  0.0 198.8 %copy-start.2 = (s32[32]{0:T(128)S(1)}, s32[32]{0:T(128)}, u32[]{:S(2)}) copy-start(s32[32]{0:T(128)} %slots.1) | copy-start | bytes 388
  0.0 201.4 %copy-start.6 = (s32[8]{0:T(128)S(1)}, s32[8]{0:T(128)}, u32[]{:S(2)}) copy-start(s32[8]{0:T(128)} %param.17) | copy-start | bytes 100
  193.1 18.7 %collective-permute-start.2 = (bf16[3,2,256,256]{3,2,1,0:T(8,128)(2,1)}, bf16[3,2,256,256]{3,2,1,0:T(8,128)(2,1)S(1)}, u32[]{:S(2)}, u32[]{:S(2)}) collective-permute-start(bf16[3,2,256,256]{3,2,1,0:T(8,128)(2,1)} %get-tuple-element.19), channel_id=1, source_target_pairs={{0,4},{1,5},{4,8},{5,9},{8,12},{9,13},{12,0},{13,1},{2,6},{3,7},{6... | collective-permute-start | bytes 2359304 | tf_op jit(solution)/shard_map/ppermute | solution.py:231
  194.5 103.5 %collective-permute-start.3 = (bf16[3,2,256,256]{3,2,1,0:T(8,128)(2,1)}, bf16[3,2,256,256]{3,2,1,0:T(8,128)(2,1)S(1)}, u32[]{:S(2)}, u32[]{:S(2)}) collective-permute-start(bf16[3,2,256,256]{3,2,1,0:T(8,128)(2,1)} %get-tuple-element.20), channel_id=1, source_target_pairs={{0,5},{1,4},{4,9},{5,8},{8,13},{9,12},{12,1},{13,0},{2,7},{3,6},{6... | collective-permute-start | bytes 2359304 | tf_op jit(solution)/shard_map/ppermute | solution.py:231
  195.2 102.8 %collective-permute-start.4 = (bf16[3,2,256,256]{3,2,1,0:T(8,128)(2,1)}, bf16[3,2,256,256]{3,2,1,0:T(8,128)(2,1)S(1)}, u32[]{:S(2)}, u32[]{:S(2)}) collective-permute-start(bf16[3,2,256,256]{3,2,1,0:T(8,128)(2,1)} %get-tuple-element.21), channel_id=1, source_target_pairs={{0,12},{1,13},{4,0},{5,1},{8,4},{9,5},{12,8},{13,9},{2,14},{3,15},... | collective-permute-start | bytes 2359304 | tf_op jit(solution)/shard_map/ppermute | solution.py:231
  196.8 101.2 %collective-permute-start.5 = (bf16[3,2,256,256]{3,2,1,0:T(8,128)(2,1)}, bf16[3,2,256,256]{3,2,1,0:T(8,128)(2,1)}, u32[]{:S(2)}, u32[]{:S(2)}) collective-permute-start(bf16[3,2,256,256]{3,2,1,0:T(8,128)(2,1)} %get-tuple-element.22), channel_id=1, source_target_pairs={{0,13},{1,12},{4,1},{5,0},{8,5},{9,4},{12,9},{13,8},{2,15},{3,14},... | collective-permute-start | bytes 2359304 | tf_op jit(solution)/shard_map/ppermute | solution.py:231
  196.8 17.1 %collective-permute-start.6 = (bf16[3,2,256,256]{3,2,1,0:T(8,128)(2,1)}, bf16[3,2,256,256]{3,2,1,0:T(8,128)(2,1)}, u32[]{:S(2)}, u32[]{:S(2)}) collective-permute-start(bf16[3,2,256,256]{3,2,1,0:T(8,128)(2,1)} %get-tuple-element.24), channel_id=1, source_target_pairs={{0,1},{1,0},{4,5},{5,4},{8,9},{9,8},{12,13},{13,12},{2,3},{3,2},{6... | collective-permute-start | bytes 2359304 | tf_op jit(solution)/shard_map/ppermute | solution.py:231
  211.8 138.4 %collective-permute-start = (bf16[3,2,256,256]{3,2,1,0:T(8,128)(2,1)}, bf16[3,2,256,256]{3,2,1,0:T(8,128)(2,1)S(1)}, u32[]{:S(2)}, u32[]{:S(2)}) collective-permute-start(bf16[3,2,256,256]{3,2,1,0:T(8,128)(2,1)} %get-tuple-element.17), channel_id=1, source_target_pairs={{0,8},{1,9},{4,12},{5,13},{8,0},{9,1},{12,4},{13,5},{2,10},{3,11},... | collective-permute-start | bytes 2359304 | tf_op jit(solution)/shard_map/ppermute | solution.py:231
  213.9 136.3 %collective-permute-start.1 = (bf16[3,2,256,256]{3,2,1,0:T(8,128)(2,1)}, bf16[3,2,256,256]{3,2,1,0:T(8,128)(2,1)S(1)}, u32[]{:S(2)}, u32[]{:S(2)}) collective-permute-start(bf16[3,2,256,256]{3,2,1,0:T(8,128)(2,1)} %get-tuple-element.18), channel_id=1, source_target_pairs={{0,9},{1,8},{4,13},{5,12},{8,1},{9,0},{12,5},{13,4},{2,11},{3,10},... | collective-permute-start | bytes 2359304 | tf_op jit(solution)/shard_map/ppermute | solution.py:231
  217.0 1.1 copy-start.1
  298.0 0.9 copy-start.3
  298.0 1.2 copy-start.4
  350.2 0.9 copy-start.5
